TPU v7x, 32 devices: a whole 2x2x4 slice. The times are simulated.
32 devices in a mesh: req: 8 (over y, x, core), tp: 4 (over z).
Axes of the slice: x: 2, y: 2, z: 4, core: 2. Of those that a mesh axis runs over, the one named last changes fastest.
Arguments:
- activations: bfloat16 [2048, 2304], P('req'), may hold values from -6 to 6
- lengths: int32 [8, 4], P('req'), may hold values from 1 to 192, 256 in all within a row
- adapter_of: int32 [8, 4], P('req'), may hold values from 0 to 15
- slot_of: int32 [16], replicated, may hold values from 0 to 15, as said below
- page_table: int32 [8, 6], P('req'), may hold values from 0 to 5, each once within a row
- experts_of: int32 [2048, 2], P('req'), may hold values from 0 to 7, all different within a row; in each aligned block of 256 rows (0 to 255, 256 to 511, ...) at most 72 rows name the same one
- attn_gain: float32 [2304], replicated, may hold values from 0.25 to 1.75
- moe_gain: float32 [2304], replicated, may hold values from 0.25 to 1.75
- w_qkv: bfloat16 [2304, 3, 2304], P(None, None, 'tp'), may hold values from -4 to 4
- output_weight: bfloat16 [2304, 2304], P('tp'), may hold values from -0.125 to 0.125
- router: bfloat16 [2304, 8], replicated, may hold values from -0.125 to 0.125
- w_gate_up: bfloat16 [8, 2304, 2, 5760], P('req', None, None, 'tp'), may hold values from -0.125 to 0.125
- w_down: bfloat16 [8, 5760, 2304], P('req', 'tp'), may hold values from -0.078125 to 0.078125
- expert_up_factors: bfloat16 [8, 256, 2, 5760], P('req', None, None, 'tp'), may hold values from -0.59765625 to 0.59765625
- pool_a: bfloat16 [16, 2304, 64], P('req'), may hold values from -0.125 to 0.125
- slot_query_key_value_up: bfloat16 [16, 16, 3, 2304], P('req', None, None, 'tp'), may hold values from -0.59765625 to 0.59765625
- pool_aout: bfloat16 [16, 2304, 16], P('req', 'tp'), may hold values from -0.125 to 0.125
- pool_bout: bfloat16 [16, 16, 2304], P('req'), may hold values from -1.796875 to 1.796875
Outputs:
- layer_out: bfloat16 [2048, 2304], P('req')
- page_cache: bfloat16 [48, 128, 2, 2304], P('req', None, None, 'tp')
Inputs may be any that keep to these rules, and one draw needn't show every extreme that they name: `slot_of`: distinct slots. `page_table`: each row holds every page index once. `experts_of`: the two experts of a token differ; among the 256 tokens of one index of req at most 72 choose one expert, and some expert reaches 72.
All inputs are finite; a program needn't handle non-finite values.
Results may differ from a plain program's by a relative error of at most 0.0095.
Values may be sent and summed in bfloat16 or wider, within the bound.
A program may use at most 128 MiB of HBM per device.

v0:
```python
import math
import jax
import jax.numpy as jnp
from jax import lax
from jax.sharding import PartitionSpec as P

D = 2304
HEAD_SIZE = 64
EXPERTS = 8
ADAPTER_RANK = 16
ADAPTER_TOTAL = 16
PAGE = 128
CAP = 72
epsilon = 1e-05
adapter_scale = 2.0
rope_base = 10000.0


def rms_norm(values, scales):
    mean_sq = jnp.mean(values * values, axis=-1, keepdims=True)
    return values * lax.rsqrt(mean_sq + epsilon) * scales


def token_layout(lengths_row, tok_count):
    ends_at = jnp.cumsum(lengths_row)
    starts = ends_at - lengths_row
    places = jnp.arange(tok_count, dtype=jnp.int32)
    request = jnp.sum((places[:, None] >= ends_at[None, :]).astype(jnp.int32), axis=1)
    position = places - starts[request]
    return (request, position)


def rotate(values, position):
    head_dim = values.shape[-1]
    half_dim = head_dim // 2
    frequency = rope_base ** (-jnp.arange(half_dim, dtype=jnp.float32) * 2.0 / head_dim)
    angles = position.astype(jnp.float32)[:, None] * frequency[None, :]
    cosine = jnp.cos(angles)[:, None, :]
    sine_part = jnp.sin(angles)[:, None, :]
    front_half = values[..., :half_dim]
    back_half = values[..., half_dim:]
    return jnp.concatenate(
        [front_half * cosine - back_half * sine_part, back_half * cosine + front_half * sine_part],
        axis=-1,
    )


def per_device(
    activations,
    lengths,
    adapter_of,
    slot_of,
    page_table,
    experts_of,
    attn_gain,
    moe_gain,
    w_qkv,
    output_weight,
    router,
    w_gate_up,
    w_down,
    expert_up_factors,
    pool_a,
    slot_query_key_value_up,
    pool_aout,
    pool_bout,
):
    token_share = activations.shape[0]
    n_req = lax.axis_size("req")
    request, position = token_layout(lengths[0], token_share)
    adapter = adapter_of[0][request]
    token_slot = slot_of[adapter]
    pool_down, slot_up_factors, pool_head, pool_outup = (
        lax.all_gather(pool_a, "req", axis=0, tiled=True),
        lax.all_gather(slot_query_key_value_up, "req", axis=0, tiled=True),
        lax.all_gather(pool_aout, "req", axis=0, tiled=True),
        lax.all_gather(pool_bout, "req", axis=0, tiled=True),
    )
    slot_count = pool_down.shape[0]
    slot_hot = token_slot[:, None] == jnp.arange(slot_count, dtype=jnp.int32)[None, :]
    head_width = w_qkv.shape[2]
    heads_number = head_width // HEAD_SIZE
    normed = rms_norm(activations.astype(jnp.float32), attn_gain).astype(jnp.bfloat16)
    down_all = jnp.einsum(
        "td,sdr->tsr",
        normed,
        pool_down[:, :, : 3 * ADAPTER_RANK],
        preferred_element_type=jnp.float32,
    )
    coeff_qkv = jnp.sum(jnp.where(slot_hot[:, :, None], down_all, 0.0), axis=1).astype(jnp.bfloat16)
    spread_rows = jnp.where(
        slot_hot[:, :, None, None],
        coeff_qkv.reshape(token_share, 1, 3, ADAPTER_RANK),
        jnp.zeros((), jnp.bfloat16),
    )
    adapter_query_key_value = jnp.einsum(
        "qwxv,wvxd->qxd", spread_rows, slot_up_factors, preferred_element_type=jnp.float32
    )
    plain_query_key_value = jnp.dot(
        normed, w_qkv.reshape(D, 3 * head_width), preferred_element_type=jnp.float32
    ).reshape(token_share, 3, head_width)
    projection_result = (plain_query_key_value + adapter_scale * adapter_query_key_value).reshape(
        token_share, 3, heads_number, HEAD_SIZE
    )
    queries = rotate(projection_result[:, 0], position).astype(jnp.bfloat16)
    keys_roped = rotate(projection_result[:, 1], position).astype(jnp.bfloat16)
    values = projection_result[:, 2].astype(jnp.bfloat16)
    pool_dev = page_table.shape[1]
    pages_used = (lengths[0] + PAGE - 1) // PAGE
    first_page = jnp.cumsum(pages_used) - pages_used
    local_page = page_table[0][first_page[request] + position // PAGE]
    cache_row = local_page * PAGE + position % PAGE
    place_hot = (
        jnp.arange(pool_dev * PAGE, dtype=jnp.int32)[:, None] == cache_row[None, :]
    ).astype(jnp.bfloat16)
    key_value = jnp.stack(
        [keys_roped.reshape(token_share, head_width), values.reshape(token_share, head_width)],
        axis=1,
    ).reshape(token_share, 2 * head_width)
    page_cache = (
        jnp.dot(place_hot, key_value, preferred_element_type=jnp.float32)
        .astype(jnp.bfloat16)
        .reshape(pool_dev, PAGE, 2, head_width)
    )
    scores = jnp.einsum("qhd,khd->hqk", queries, keys_roped, preferred_element_type=jnp.float32) * (
        1.0 / math.sqrt(HEAD_SIZE)
    )
    allowed = (request[:, None] == request[None, :]) & (position[None, :] <= position[:, None])
    scores = jnp.where(allowed[None], scores, -1e30)
    row_max = jnp.max(scores, axis=-1, keepdims=True)
    weights = jnp.exp(scores - row_max)
    weights = (weights / jnp.sum(weights, axis=-1, keepdims=True)).astype(jnp.bfloat16)
    attention_result = (
        jnp.einsum("hqk,khd->qhd", weights, values, preferred_element_type=jnp.float32)
        .astype(jnp.bfloat16)
        .reshape(token_share, head_width)
    )
    aout_all = jnp.einsum(
        "tc,scr->tsr", attention_result, pool_head, preferred_element_type=jnp.float32
    )
    coeff_out = jnp.sum(jnp.where(slot_hot[:, :, None], aout_all, 0.0), axis=1)
    spread_out = jnp.where(slot_hot[:, :, None], coeff_out[:, None, :], 0.0).reshape(
        token_share, slot_count * ADAPTER_RANK
    )
    output_update = jnp.dot(
        spread_out,
        pool_outup.astype(jnp.float32).reshape(slot_count * ADAPTER_RANK, D),
        precision=lax.Precision.HIGHEST,
    )
    head_term = (
        jnp.dot(attention_result, output_weight, preferred_element_type=jnp.float32)
        + adapter_scale * output_update
    )
    mixed_out = lax.psum(head_term, "tp")
    residual_stream = activations.astype(jnp.float32) + mixed_out
    normed_moe = rms_norm(residual_stream, moe_gain).astype(jnp.bfloat16)
    logits = jnp.dot(normed_moe, router, preferred_element_type=jnp.float32)
    chosen = jnp.take_along_axis(logits, experts_of, axis=1)
    gate_weights = 1.0 / (1.0 + jnp.exp(chosen[:, ::-1] - chosen))
    exp_all = jnp.einsum(
        "td,sdr->tsr",
        normed_moe,
        pool_down[:, :, 3 * ADAPTER_RANK :],
        preferred_element_type=jnp.float32,
    )
    coeff_exp = jnp.sum(jnp.where(slot_hot[:, :, None], exp_all, 0.0), axis=1).astype(jnp.bfloat16)
    capacity = CAP
    split_count = n_req // EXPERTS
    flat_expert = experts_of.reshape(-1)
    expert_hot = (flat_expert[:, None] == jnp.arange(EXPERTS, dtype=jnp.int32)[None, :]).astype(
        jnp.int32
    )
    order_in = jnp.sum((jnp.cumsum(expert_hot, axis=0) - expert_hot) * expert_hot, axis=1)
    column = flat_expert * capacity + order_in
    pick = (column[:, None] == jnp.arange(EXPERTS * capacity, dtype=jnp.int32)[None, :]).reshape(
        token_share, 2, EXPERTS * capacity
    )
    route = jnp.any(pick, axis=1).astype(jnp.bfloat16)
    combine_weights = jnp.sum(jnp.where(pick, gate_weights[:, :, None], 0.0), axis=1)

    def spread_copies(array):
        shaped = array.reshape((EXPERTS, 1, capacity) + array.shape[1:])
        return jnp.broadcast_to(shaped, (EXPERTS, split_count, capacity) + array.shape[1:]).reshape(
            (n_req, capacity) + array.shape[1:]
        )

    send_coeff = jnp.einsum(
        "ts,tr->sr", route, coeff_exp, preferred_element_type=jnp.float32
    ).astype(jnp.bfloat16)
    send_ids = jnp.einsum(
        "ts,t->s", route, adapter.astype(jnp.bfloat16), preferred_element_type=jnp.float32
    ).astype(jnp.bfloat16)
    adapter_range = jnp.arange(ADAPTER_TOTAL, dtype=jnp.int32).astype(jnp.bfloat16)
    send_rows = jnp.einsum(
        "ts,td->sd", route, normed_moe, preferred_element_type=jnp.float32
    ).astype(jnp.bfloat16)
    expert_input_rows = lax.all_to_all(
        spread_copies(send_rows), "req", split_axis=0, concat_axis=0, tiled=True
    )
    coeff_rank = lax.all_to_all(
        spread_copies(send_coeff), "req", split_axis=0, concat_axis=0, tiled=True
    )
    adapter_ids = lax.all_to_all(
        spread_copies(send_ids), "req", split_axis=0, concat_axis=0, tiled=True
    )
    count = expert_input_rows.shape[1]
    flat_rows = expert_input_rows.reshape(n_req * count, D)
    flat_coeff = coeff_rank.reshape(n_req * count, ADAPTER_RANK)
    flat_ids = adapter_ids.reshape(n_req * count)
    unit_count = w_gate_up.shape[3]
    broad_coefficients = jnp.where(
        flat_ids[:, None, None] == adapter_range[None, :, None],
        flat_coeff[:, None, :],
        jnp.zeros((), jnp.bfloat16),
    ).reshape(n_req * count, ADAPTER_TOTAL * ADAPTER_RANK)
    before_norm = jnp.dot(
        flat_rows, w_gate_up[0].reshape(D, 2 * unit_count), preferred_element_type=jnp.float32
    )
    before_norm = before_norm + adapter_scale * jnp.dot(
        broad_coefficients,
        expert_up_factors[0].reshape(ADAPTER_TOTAL * ADAPTER_RANK, 2 * unit_count),
        preferred_element_type=jnp.float32,
    )
    hidden = (jax.nn.silu(before_norm[:, :unit_count]) * before_norm[:, unit_count:]).astype(
        jnp.bfloat16
    )
    partial_term = jnp.dot(hidden, w_down[0], preferred_element_type=jnp.float32).astype(
        jnp.bfloat16
    )
    returned = lax.all_to_all(
        partial_term.reshape(n_req, count, D), "req", split_axis=0, concat_axis=0, tiled=True
    )
    summed = jnp.sum(
        returned.astype(jnp.float32).reshape(EXPERTS, split_count, capacity, D), axis=1
    ).reshape(EXPERTS * capacity, D)
    moe_part = jnp.dot(combine_weights, summed, precision=lax.Precision.HIGHEST)
    moe_sum = lax.psum(moe_part.astype(jnp.bfloat16), "tp").astype(jnp.float32)
    layer_out = (residual_stream + moe_sum).astype(jnp.bfloat16)
    return (layer_out, page_cache)


def solution(mesh):
    return jax.shard_map(
        per_device,
        mesh=mesh,
        in_specs=(
            P("req", None),
            P("req", None),
            P("req", None),
            P(),
            P("req", None),
            P("req", None),
            P(),
            P(),
            P(None, None, "tp"),
            P("tp", None),
            P(),
            P("req", None, None, "tp"),
            P("req", "tp", None),
            P("req", None, None, "tp"),
            P("req", None, None),
            P("req", None, None, "tp"),
            P("req", "tp", None),
            P("req", None, None),
        ),
        out_specs=(P("req", None), P("req", None, None, "tp")),
        check_vma=False,
    )
```

profile of v0, /device:TPU:0, one launch (start us, length us, event | category | flops | bytes accessed | tf_op | source)
XLA Modules:
  0.0 364.0 jit_solution(4491412793175182737)
XLA Ops:
  17.8 6.8 %compare_select_fusion.9 = (s32[256,1]{0,1:T(1,128)S(1)}, s32[256,1]{0,1:T(1,128)S(1)}, s32[256,1]{0,1:T(1,128)S(1)}) fusion(s32[]{:T(128)} %bitcast.20, s32[]{:T(128)} %bitcast.21, s32[]{:T(128)} %bitcast.22, s32[]{:T(128)} %bitcast.23, s32[]{:T(128)} %bitcast.24, s32[]{:T(128)} %bitcast.26, s32[]{:T(128)} %bitcast.25, s32[]{:T(128)} %bitcast.10, ...), kind=kLoop, calls=%fused_computation.105 | loop fusion | flops 6144 | bytes 4140 | tf_op jit(solution)/shard_map/gather | solution.py:72
  24.6 5.7 %select_select_fusion.2 = s32[256]{0:T(256)S(1)} fusion(pred[256]{0:T(512)(128)(4,1)S(1)} %get-tuple-element.22, pred[256]{0:T(512)(128)(4,1)S(1)} %get-tuple-element.21, pred[256]{0:T(512)(128)(4,1)S(1)} %get-tuple-element.20, pred[256]{0:T(512)(128)(4,1)S(1)} %get-tuple-element.19, pred[256]{0:T(512)(128)(4,1)S(1)} %get-tuple-element.18, ...), kind=kLoop, calls=%fused_computation.137 | loop fusion | flops 2304 | bytes 4388 | tf_op jit(solution)/shard_map/gather | solution.py:72
  31.0 8.8 %fusion.49 = (s32[256,1]{0,1:T(1,128)S(1)}, s32[256,1]{0,1:T(1,128)S(1)}) fusion(s32[]{:T(128)} %bitcast.71, s32[]{:T(128)} %bitcast.72, s32[]{:T(128)} %bitcast.73, s32[]{:T(128)} %bitcast.67, s32[]{:T(128)} %bitcast.74, s32[]{:T(128)} %bitcast.68, s32[]{:T(128)} %bitcast.76, s32[]{:T(128)} %bitcast.75, s32[]{:T(128)} %bitcast.70, s32[]{:T(128)} %bitcast.69, ...), kind=kLoop, calls=%fused_computation.132 | loop fusion | flops 11008 | bytes 3128 | tf_op jit(solution)/shard_map/mul | solution.py:112
  40.0 12.0 %all_gather.14 = bf16[16,576,16]{1,2,0:T(8,128)(2,1)S(1)} all-gather(bf16[2,576,16]{1,2,0:T(8,128)(2,1)} %param.34), channel_id=1, replica_groups=mesh['req'=8,'tp'=4] {'req'}, dimensions={0}, use_global_device_ids=true | all-gather | bytes 331776 | tf_op jit(solution)/shard_map/all_gather | solution.py:76
  52.0 12.0 %all_gather.13 = bf16[16,16,3,576]{3,1,2,0:T(8,128)(2,1)} all-gather(bf16[2,16,3,576]{3,1,2,0:T(8,128)(2,1)S(1)} %copy-done.14), channel_id=1, replica_groups=mesh['req'=8,'tp'=4] {'req'}, dimensions={0}, use_global_device_ids=true | all-gather | bytes 995328 | tf_op jit(solution)/shard_map/all_gather | solution.py:75
  64.2 6.8 %fusion.1 = f32[256,3,576]{0,2,1:T(8,128)} fusion(bf16[2304,3,576]{0,2,1:T(8,128)(2,1)} %param.26, bf16[256,2304]{1,0:T(8,128)(2,1)S(1)} %copy-done.5, f32[2304]{0:T(1024)S(1)} %copy-done.18, f32[256]{0:T(256)S(1)} %add_rsqrt_fusion.1), kind=kOutput, calls=%fused_computation.2 | convolution fusion | flops 2040791040 | bytes 10921984 | tf_op jit(solution)/shard_map/dot_general | solution.py:99
  78.1 3.4 fusion.67
  86.5 2.6 convolution_add_fusion
  93.1 3.4 all-to-all-start.1
  96.6 88.4 %all-reduce.3.cloned.1.call-done = f32[256,2304]{1,0:T(8,128)} async-done(((f32[256,2304]{1,0:T(8,128)}), f32[256,2304]{1,0:T(8,128)}) %all-reduce.3.cloned.1.call-update) | async-done | bytes 2359312 | tf_op jit(solution)/shard_map/psum | solution.py:154
  190.9 3.7 %all-to-all-start.2 = ((bf16[8,72,16]{1,2,0:T(8,128)(2,1)}), bf16[8,72,16]{1,2,0:T(8,128)(2,1)S(1)}, u32[]{:S(2)}, u32[]{:S(2)}) async-start(bf16[8,72,16]{1,2,0:T(8,128)(2,1)} %copy.92), calls=%async_computation.2 | async-start | bytes 65536 | tf_op jit(solution)/shard_map/all_to_all | solution.py:200
  194.6 3.7 %convolution_convert_fusion = bf16[576,2304]{1,0:T(8,128)(2,1)} fusion(pred[256,576]{0,1:T(8,128)(4,1)S(1)} %fusion.17, bf16[256,2304]{1,0:T(8,128)(2,1)} %copy-done.3), kind=kOutput, calls=%fused_computation.8 | convolution fusion | flops 680804352 | bytes 3981312 | tf_op jit(solution)/shard_map/ts,td->sd/dot_general | solution.py:194
  199.4 3.6 all-to-all-start
  203.5 32.1 %all-to-all-done = bf16[8,72,2304]{2,1,0:T(8,128)(2,1)S(1)} async-done(((bf16[8,72,2304]{2,1,0:T(8,128)(2,1)}), bf16[8,72,2304]{2,1,0:T(8,128)(2,1)S(1)}, u32[]{:S(2)}, u32[]{:S(2)}) %all-to-all-start) | async-done | bytes 2654240 | tf_op jit(solution)/shard_map/all_to_all | solution.py:197
  235.6 11.4 %fusion.72 = f32[576,2880]{1,0:T(8,128)S(1)} fusion(bf16[576,2304]{1,0:T(8,128)(2,1)S(1)} %bitcast.153, bf16[2304,2880]{0,1:T(8,128)(2,1)} %bitcast.173), kind=kOutput, calls=%fused_computation.165 | convolution fusion | flops 7644119040 | bytes 22560768 | tf_op jit(solution)/shard_map/dot_general | solution.py:216
  248.3 9.2 %fusion.5 = bf16[576,2304]{1,0:T(8,128)(2,1)} fusion(bf16[1,1440,2304]{2,1,0:T(8,128)(2,1)} %param.30, f32[576,2880]{1,0:T(8,128)S(1)} %multiply_add_fusion), kind=kOutput, calls=%fused_computation.7 | convolution fusion | flops 3828363264 | bytes 16367616 | tf_op jit(solution)/shard_map/dot_general | solution.py:227
  257.5 4.5 %all-to-all-start.3 = ((bf16[8,72,2304]{2,1,0:T(8,128)(2,1)}), bf16[8,72,2304]{2,1,0:T(8,128)(2,1)}, u32[]{:S(2)}, u32[]{:S(2)}) async-start(bf16[8,72,2304]{2,1,0:T(8,128)(2,1)} %bitcast.152), calls=%async_computation.3 | async-start | bytes 5308416 | tf_op jit(solution)/shard_map/all_to_all | solution.py:230
  263.0 3.6 gather_fusion
  267.1 27.5 %all-to-all-done.3 = bf16[8,72,2304]{2,1,0:T(8,128)(2,1)} async-done(((bf16[8,72,2304]{2,1,0:T(8,128)(2,1)}), bf16[8,72,2304]{2,1,0:T(8,128)(2,1)}, u32[]{:S(2)}, u32[]{:S(2)}) %all-to-all-start.3) | async-done | bytes 2654240 | tf_op jit(solution)/shard_map/all_to_all | solution.py:230
  294.6 5.9 %convolution_convert_fusion.1 = bf16[256,2304]{1,0:T(8,128)(2,1)} fusion(f32[256,576]{0,1:T(8,128)S(1)} %select_reduce_fusion, bf16[576,2304]{1,0:T(8,128)(2,1)} %bitcast.65), kind=kOutput, calls=%fused_computation.12 | convolution fusion | flops 4077453312 | bytes 4423680 | tf_op jit(solution)/shard_map/dot_general | solution.py:236
  302.5 3.0 reshape.581
  305.5 6.7 %copy.94 = bf16[6,128,2,576]{1,3,2,0:T(8,128)(2,1)} copy(bf16[6,128,2,576]{3,2,1,0:T(2,128)(2,1)} %reshape.581) | data formatting | bytes 3538944
  312.2 41.7 %all-reduce.5.cloned.1.call-done = bf16[256,2304]{1,0:T(8,128)(2,1)} async-done(((bf16[256,2304]{1,0:T(8,128)(2,1)}), bf16[256,2304]{1,0:T(8,128)(2,1)}) %all-reduce.5.cloned.1.call-update) | async-done | bytes 1179664 | tf_op jit(solution)/shard_map/psum | solution.py:237
  353.8 3.7 %add_convert_fusion = bf16[256,2304]{1,0:T(8,128)(2,1)} fusion(bf16[256,2304]{1,0:T(8,128)(2,1)} %all-reduce.5.cloned.1.call-done, f32[256,2304]{1,0:T(8,128)} %all-reduce.3.cloned.1.call-done, bf16[256,2304]{1,0:T(8,128)(2,1)} %param.18), kind=kLoop, calls=%fused_computation.22 | loop fusion | flops 2949120 | bytes 5898240 | tf_op jit(solution)/shard_map/convert_element_type | solution.py:238
  (126 shorter events, 39.8 us)
Async XLA Ops:
  7.2 79.4 %copy-start = (bf16[576,2304]{1,0:T(8,128)(2,1)S(1)}, bf16[576,2304]{1,0:T(8,128)(2,1)}, u32[]{:S(2)}) copy-start(bf16[576,2304]{1,0:T(8,128)(2,1)} %param.27) | copy-start | bytes 7962628
  7.2 44.8 %copy-start.14 = (bf16[2,16,3,576]{3,1,2,0:T(8,128)(2,1)S(1)}, bf16[2,16,3,576]{3,1,2,0:T(8,128)(2,1)}, u32[]{:S(2)}) copy-start(bf16[2,16,3,576]{3,1,2,0:T(8,128)(2,1)} %param.33) | copy-start | bytes 331780
  7.2 57.0 %copy-start.18 = (f32[2304]{0:T(1024)S(1)}, f32[2304]{0:T(1024)}, u32[]{:S(2)}) copy-start(f32[2304]{0:T(1024)} %param.24) | copy-start | bytes 27652
  7.2 63.8 %all-gather.3.cloned.1.call-start = ((), (), s32[]{:S(2)}) async-start(), calls=%async_computation.4 | async-start | bytes 5308416 | tf_op jit(solution)/shard_map/all_gather | solution.py:74
  7.9 76.1 %all-gather.5.cloned.1.call-start = ((), (), s32[]{:S(2)}) async-start(), calls=%async_computation.5 | async-start | bytes 1327104 | tf_op jit(solution)/shard_map/all_gather | solution.py:77
  8.7 176.3 %all-reduce.3.cloned.1.call-start = ((), (), s32[]{:S(2)}) async-start(), calls=%async_computation.6 | async-start | bytes 4718592 | tf_op jit(solution)/shard_map/psum | solution.py:154
  10.4 53.8 %copy-start.5 = (bf16[256,2304]{1,0:T(8,128)(2,1)S(1)}, bf16[256,2304]{1,0:T(8,128)(2,1)}, u32[]{:S(2)}) copy-start(bf16[256,2304]{1,0:T(8,128)(2,1)} %param.18) | copy-start | bytes 3538948
  71.0 1.5 copy-start.6
  71.0 2.5 slice-start
  73.6 1.8 copy-start.10
  78.1 3.4 copy-start.12
  93.1 97.8 %all-to-all-start.1 = ((bf16[8,1,72]{2,1,0:T(2,128)(2,1)}), bf16[8,1,72]{2,1,0:T(2,128)(2,1)S(1)}, u32[]{:S(2)}, u32[]{:S(2)}) async-start(bf16[8,1,72]{2,1,0:T(2,128)(2,1)} %all_to_all.20), calls=%async_computation.1 | async-start | bytes 8192 | tf_op jit(solution)/shard_map/all_to_all | solution.py:203
  96.6 90.9 %copy-start.17 = (f32[2304]{0:T(1024)S(1)}, f32[2304]{0:T(1024)}, u32[]{:S(2)}) copy-start(f32[2304]{0:T(1024)} %param.25) | copy-start | bytes 27652
  185.0 2.7 copy-start.2
  185.0 3.0 copy-start.7
  190.9 8.5 %all-to-all-start.2 = ((bf16[8,72,16]{1,2,0:T(8,128)(2,1)}), bf16[8,72,16]{1,2,0:T(8,128)(2,1)S(1)}, u32[]{:S(2)}, u32[]{:S(2)}) async-start(bf16[8,72,16]{1,2,0:T(8,128)(2,1)} %copy.92), calls=%async_computation.2 | async-start | bytes 65536 | tf_op jit(solution)/shard_map/all_to_all | solution.py:200
  199.4 36.2 %all-to-all-start = ((bf16[8,72,2304]{2,1,0:T(8,128)(2,1)}), bf16[8,72,2304]{2,1,0:T(8,128)(2,1)S(1)}, u32[]{:S(2)}, u32[]{:S(2)}) async-start(bf16[8,72,2304]{2,1,0:T(8,128)(2,1)} %bitcast.55), calls=%async_computation | async-start | bytes 5308416 | tf_op jit(solution)/shard_map/all_to_all | solution.py:197
  235.6 11.4 %copy-start.11 = (bf16[1,256,2,1440]{1,3,2,0:T(8,128)(2,1)S(1)}, bf16[1,256,2,1440]{1,3,2,0:T(8,128)(2,1)}, u32[]{:S(2)}) copy-start(bf16[1,256,2,1440]{1,3,2,0:T(8,128)(2,1)} %param.31) | copy-start | bytes 4423684
  257.5 5.1 %copy-start.4 = (bf16[256,2304]{1,0:T(8,128)(2,1)S(1)}, bf16[256,2304]{1,0:T(8,128)(2,1)}, u32[]{:S(2)}) copy-start(bf16[256,2304]{1,0:T(8,128)(2,1)} %copy-done.3) | copy-start | bytes 3538948
  257.5 5.1 %copy-start.15 = (bf16[2304,8]{0,1:T(8,128)(2,1)S(1)}, bf16[2304,8]{0,1:T(8,128)(2,1)}, u32[]{:S(2)}) copy-start(bf16[2304,8]{0,1:T(8,128)(2,1)} %param.28) | copy-start | bytes 110596
  257.5 37.1 %all-to-all-start.3 = ((bf16[8,72,2304]{2,1,0:T(8,128)(2,1)}), bf16[8,72,2304]{2,1,0:T(8,128)(2,1)}, u32[]{:S(2)}, u32[]{:S(2)}) async-start(bf16[8,72,2304]{2,1,0:T(8,128)(2,1)} %bitcast.152), calls=%async_computation.3 | async-start | bytes 5308416 | tf_op jit(solution)/shard_map/all_to_all | solution.py:230
  262.0 91.8 %all-reduce.5.cloned.1.call-start = ((), (), s32[]{:S(2)}) async-start(), calls=%async_computation.7 | async-start | bytes 2359296 | tf_op jit(solution)/shard_map/psum | solution.py:237
  294.6 7.0 %copy-start.13 = (bf16[256,9,32]{0,2,1:T(8,128)(2,1)S(1)}, bf16[256,9,32]{0,2,1:T(8,128)(2,1)}, u32[]{:S(2)}) copy-start(bf16[256,9,32]{0,2,1:T(8,128)(2,1)} %copy-done.12) | copy-start | bytes 442372
  305.5 52.0 %copy-start.1 = (bf16[576,2304]{1,0:T(8,128)(2,1)S(1)}, bf16[576,2304]{1,0:T(8,128)(2,1)}, u32[]{:S(2)}) copy-start(bf16[576,2304]{1,0:T(8,128)(2,1)} %param.27) | copy-start | bytes 7962628
  (5 other events, 5.6 us)
Sparse Core Ops, SparseCore 0:
  9.9 42.8 all-gather.2
  54.7 24.0 all-gather.4
  89.3 95.5 all-reduce.2
  300.6 53.1 all-reduce.4
where the time goes:
time: 365 us; the launch traced here: 364 us
  waiting for transfers between devices  192 us (53%)
  matrix products  52.9 us (14%)
  other arithmetic  35.5 us (10%)
  local copies, waits for them, and re-layouts  29.5 us (8%)
  blocking collectives  24 us (7%)
  starting transfers between devices  15.6 us (4%)
  between operations  14.2 us (4%)
    psum x1, waiting for transfers between devices, per_device(): mixed_out = lax.psum(head_term, 'tp')  88.4 us
    psum x1, waiting for transfers between devices, per_device(): moe_sum = lax.psum(moe_part.astype(jnp.bfloat16), 'tp').astype(jnp.float32)  41.7 us
    all_to_all x1, waiting for transfers between devices, per_device(): lax.all_to_all(spread_copies(send_rows), 'req', split_axis=0, concat_axis...  32.1 us
    all_to_all x1, waiting for transfers between devices, per_device(): lax.all_to_all(partial_term.reshape(n_req, count, D), 'req', split_axis=0...  27.5 us
    gather x3, other arithmetic, per_device(): token_slot = slot_of[adapter]  12.5 us
    unnamed x40, local copies, waits for them, and re-layouts  12.2 us
    all_gather x1, blocking collectives, per_device(): lax.all_gather(pool_aout, 'req', axis=0, tiled=True)  12 us
    all_gather x1, blocking collectives, per_device(): lax.all_gather(slot_query_key_value_up, 'req', axis=0, tiled=True)  12 us
  transfers between devices with their start and end apart: 8, of which 5 were waited for; matrix products, arithmetic and copies ran while one was open for 20% of the time, Pallas kernels for 0%

commit v1 on v0

--- a/solution.py
+++ b/solution.py
@@ -3,6 +3,7 @@
 import jax.numpy as jnp
 from jax import lax
 from jax.sharding import PartitionSpec as P
+from jax.lax import axis_size, ppermute
 
 D = 2304
 HEAD_SIZE = 64
@@ -65,6 +66,17 @@
     pool_aout,
     pool_bout,
 ):
+
+    def _press_kinds(local_block, a_name):
+        n_all = axis_size(a_name)
+        piece_out = local_block
+        for dev in [
+            [(idx, idx ^ ii) for idx in range(n_all)] for ii in (1, 2, 4, 8, 16) if ii < n_all
+        ]:
+            v_next = ppermute(piece_out, a_name, dev)
+            piece_out = piece_out + v_next
+        return piece_out
+
     token_share = activations.shape[0]
     n_req = lax.axis_size("req")
     request, position = token_layout(lengths[0], token_share)
@@ -151,7 +163,7 @@
         jnp.dot(attention_result, output_weight, preferred_element_type=jnp.float32)
         + adapter_scale * output_update
     )
-    mixed_out = lax.psum(head_term, "tp")
+    mixed_out = _press_kinds(head_term, "tp")
     residual_stream = activations.astype(jnp.float32) + mixed_out
     normed_moe = rms_norm(residual_stream, moe_gain).astype(jnp.bfloat16)
     logits = jnp.dot(normed_moe, router, preferred_element_type=jnp.float32)

time: 365 us -> 428 us (1.17)
  waiting for transfers between devices: 192 us -> 253 us
    ppermute x0 -> x2, waiting for transfers between devices: none -> 147 us  [_press_kinds(): v_next = ppermute(piece_out, a_name, dev)]
    psum x1 -> x0, waiting for transfers between devices: 88.4 us -> none  [per_device(): mixed_out = lax.psum(head_term, 'tp')]
  transfers between devices with their start and end apart: 8 -> 9, of which waited for: 5 -> 6; matrix products, arithmetic and copies ran while one was open for 20% -> 18% of each run, Pallas kernels for 0% -> 0%
where the time goes in v1:
time: 428 us; the launch traced here: 427 us
  waiting for transfers between devices  253 us (59%)
  matrix products  51.4 us (12%)
  other arithmetic  35.7 us (8%)
  local copies, waits for them, and re-layouts  29.2 us (7%)
  blocking collectives  24 us (6%)
  starting transfers between devices  19.4 us (5%)
  between operations  14.3 us (3%)
    ppermute x2, waiting for transfers between devices, _press_kinds(): v_next = ppermute(piece_out, a_name, dev)  147 us
    psum x1, waiting for transfers between devices, per_device(): moe_sum = lax.psum(moe_part.astype(jnp.bfloat16), 'tp').astype(jnp.float32)  43.6 us
    all_to_all x1, waiting for transfers between devices, per_device(): lax.all_to_all(spread_copies(send_rows), 'req', split_axis=0, concat_axis...  32.1 us
    all_to_all x1, waiting for transfers between devices, per_device(): lax.all_to_all(partial_term.reshape(n_req, count, D), 'req', split_axis=0...  27.5 us
    gather x3, other arithmetic, per_device(): token_slot = slot_of[adapter]  12.5 us
    all_gather x1, blocking collectives, per_device(): lax.all_gather(pool_aout, 'req', axis=0, tiled=True)  12 us
    all_gather x1, blocking collectives, per_device(): lax.all_gather(slot_query_key_value_up, 'req', axis=0, tiled=True)  12 us
    dot_general x1, matrix products, per_device(): jnp.dot(flat_rows, w_gate_up[0].reshape(D, 2 * unit_count), preferred_ele...  11.4 us
  transfers between devices with their start and end apart: 9, of which 6 were waited for; matrix products, arithmetic and copies ran while one was open for 18% of the time, Pallas kernels for 0%

profile of v1, /device:TPU:0, one launch (start us, length us, event | category | flops | bytes accessed | tf_op | source)
XLA Modules:
  0.0 426.7 jit_solution(7913849905272580634)
XLA Ops:
  17.8 6.8 %compare_select_fusion.9 = (s32[256,1]{0,1:T(1,128)S(1)}, s32[256,1]{0,1:T(1,128)S(1)}, s32[256,1]{0,1:T(1,128)S(1)}) fusion(s32[]{:T(128)} %bitcast.20, s32[]{:T(128)} %bitcast.21, s32[]{:T(128)} %bitcast.22, s32[]{:T(128)} %bitcast.23, s32[]{:T(128)} %bitcast.24, s32[]{:T(128)} %bitcast.26, s32[]{:T(128)} %bitcast.25, s32[]{:T(128)} %bitcast.10, ...), kind=kLoop, calls=%fused_computation.105 | loop fusion | flops 6144 | bytes 4140 | tf_op jit(solution)/shard_map/gather | solution.py:84
  24.6 5.7 %select_select_fusion.2 = s32[256]{0:T(256)S(1)} fusion(pred[256]{0:T(512)(128)(4,1)S(1)} %get-tuple-element.22, pred[256]{0:T(512)(128)(4,1)S(1)} %get-tuple-element.21, pred[256]{0:T(512)(128)(4,1)S(1)} %get-tuple-element.20, pred[256]{0:T(512)(128)(4,1)S(1)} %get-tuple-element.19, pred[256]{0:T(512)(128)(4,1)S(1)} %get-tuple-element.18, ...), kind=kLoop, calls=%fused_computation.137 | loop fusion | flops 2304 | bytes 4388 | tf_op jit(solution)/shard_map/gather | solution.py:84
  31.0 8.8 %fusion.49 = (s32[256,1]{0,1:T(1,128)S(1)}, s32[256,1]{0,1:T(1,128)S(1)}) fusion(s32[]{:T(128)} %bitcast.71, s32[]{:T(128)} %bitcast.72, s32[]{:T(128)} %bitcast.73, s32[]{:T(128)} %bitcast.67, s32[]{:T(128)} %bitcast.74, s32[]{:T(128)} %bitcast.68, s32[]{:T(128)} %bitcast.76, s32[]{:T(128)} %bitcast.75, s32[]{:T(128)} %bitcast.70, s32[]{:T(128)} %bitcast.69, ...), kind=kLoop, calls=%fused_computation.132 | loop fusion | flops 11008 | bytes 3128 | tf_op jit(solution)/shard_map/mul | solution.py:124
  40.0 12.0 %all_gather.14 = bf16[16,576,16]{1,2,0:T(8,128)(2,1)S(1)} all-gather(bf16[2,576,16]{1,2,0:T(8,128)(2,1)} %param.34), channel_id=1, replica_groups=mesh['req'=8,'tp'=4] {'req'}, dimensions={0}, use_global_device_ids=true | all-gather | bytes 331776 | tf_op jit(solution)/shard_map/all_gather | solution.py:88
  52.0 12.0 %all_gather.13 = bf16[16,16,3,576]{3,1,2,0:T(8,128)(2,1)} all-gather(bf16[2,16,3,576]{3,1,2,0:T(8,128)(2,1)S(1)} %copy-done.14), channel_id=1, replica_groups=mesh['req'=8,'tp'=4] {'req'}, dimensions={0}, use_global_device_ids=true | all-gather | bytes 995328 | tf_op jit(solution)/shard_map/all_gather | solution.py:87
  64.2 6.8 %fusion.1 = f32[256,3,576]{0,2,1:T(8,128)} fusion(bf16[2304,3,576]{0,2,1:T(8,128)(2,1)} %param.26, bf16[256,2304]{1,0:T(8,128)(2,1)S(1)} %copy-done.7, f32[2304]{0:T(1024)S(1)} %copy-done.18, f32[256]{0:T(256)S(1)} %add_rsqrt_fusion.1), kind=kOutput, calls=%fused_computation.2 | convolution fusion | flops 2040791040 | bytes 10921984 | tf_op jit(solution)/shard_map/dot_general | solution.py:111
  78.0 3.4 fusion.67
  89.3 52.0 %collective-permute-done = f32[256,2304]{1,0:T(8,128)S(1)} collective-permute-done((f32[256,2304]{1,0:T(8,128)S(1)}, f32[256,2304]{1,0:T(8,128)S(1)}, u32[]{:S(2)}, u32[]{:S(2)}) %collective-permute-start) | collective-permute-done | bytes 2359328 | tf_op jit(solution)/shard_map/ppermute | solution.py:76
  147.3 3.5 all-to-all-start.1
  150.8 95.0 %collective-permute-done.1 = f32[256,2304]{1,0:T(8,128)} collective-permute-done((f32[256,2304]{1,0:T(8,128)S(1)}, f32[256,2304]{1,0:T(8,128)}, u32[]{:S(2)}, u32[]{:S(2)}) %collective-permute-start.1) | collective-permute-done | bytes 2359328 | tf_op jit(solution)/shard_map/ppermute | solution.py:76
  245.9 3.2 multiply_reduce_fusion
  252.6 3.3 all-to-all-start.2
  256.0 3.7 convolution_convert_fusion
  260.7 3.6 all-to-all-start
  264.8 32.1 %all-to-all-done = bf16[8,72,2304]{2,1,0:T(8,128)(2,1)S(1)} async-done(((bf16[8,72,2304]{2,1,0:T(8,128)(2,1)}), bf16[8,72,2304]{2,1,0:T(8,128)(2,1)S(1)}, u32[]{:S(2)}, u32[]{:S(2)}) %all-to-all-start) | async-done | bytes 2654240 | tf_op jit(solution)/shard_map/all_to_all | solution.py:209
  296.9 11.4 %fusion.72 = f32[576,2880]{1,0:T(8,128)S(1)} fusion(bf16[576,2304]{1,0:T(8,128)(2,1)S(1)} %bitcast.153, bf16[2304,2880]{0,1:T(8,128)(2,1)} %bitcast.173), kind=kOutput, calls=%fused_computation.165 | convolution fusion | flops 7644119040 | bytes 22560768 | tf_op jit(solution)/shard_map/dot_general | solution.py:228
  309.6 9.2 %fusion.5 = bf16[576,2304]{1,0:T(8,128)(2,1)} fusion(bf16[1,1440,2304]{2,1,0:T(8,128)(2,1)} %param.30, f32[576,2880]{1,0:T(8,128)S(1)} %multiply_add_fusion), kind=kOutput, calls=%fused_computation.7 | convolution fusion | flops 3828363264 | bytes 16367616 | tf_op jit(solution)/shard_map/dot_general | solution.py:239
  318.8 4.5 %all-to-all-start.3 = ((bf16[8,72,2304]{2,1,0:T(8,128)(2,1)}), bf16[8,72,2304]{2,1,0:T(8,128)(2,1)}, u32[]{:S(2)}, u32[]{:S(2)}) async-start(bf16[8,72,2304]{2,1,0:T(8,128)(2,1)} %bitcast.152), calls=%async_computation.3 | async-start | bytes 5308416 | tf_op jit(solution)/shard_map/all_to_all | solution.py:242
  324.3 3.6 gather_fusion
  328.4 27.5 %all-to-all-done.3 = bf16[8,72,2304]{2,1,0:T(8,128)(2,1)} async-done(((bf16[8,72,2304]{2,1,0:T(8,128)(2,1)}), bf16[8,72,2304]{2,1,0:T(8,128)(2,1)}, u32[]{:S(2)}, u32[]{:S(2)}) %all-to-all-start.3) | async-done | bytes 2654240 | tf_op jit(solution)/shard_map/all_to_all | solution.py:242
  355.9 5.9 %convolution_convert_fusion.1 = bf16[256,2304]{1,0:T(8,128)(2,1)} fusion(f32[256,576]{0,1:T(8,128)S(1)} %select_reduce_fusion, bf16[576,2304]{1,0:T(8,128)(2,1)} %bitcast.65), kind=kOutput, calls=%fused_computation.12 | convolution fusion | flops 4077453312 | bytes 4423680 | tf_op jit(solution)/shard_map/dot_general | solution.py:248
  366.8 6.7 %copy.94 = bf16[6,128,2,576]{1,3,2,0:T(8,128)(2,1)} copy(bf16[6,128,2,576]{3,2,1,0:T(2,128)(2,1)} %reshape.581) | data formatting | bytes 3538944
  373.4 43.6 %all-reduce.2.cloned.1.call-done = bf16[256,2304]{1,0:T(8,128)(2,1)} async-done(((bf16[256,2304]{1,0:T(8,128)(2,1)}), bf16[256,2304]{1,0:T(8,128)(2,1)}) %all-reduce.2.cloned.1.call-update) | async-done | bytes 1179664 | tf_op jit(solution)/shard_map/psum | solution.py:249
  417.0 3.2 add_convert_fusion
  (128 shorter events, 45.1 us)
Async XLA Ops:
  7.2 79.3 %copy-start = (bf16[576,2304]{1,0:T(8,128)(2,1)S(1)}, bf16[576,2304]{1,0:T(8,128)(2,1)}, u32[]{:S(2)}) copy-start(bf16[576,2304]{1,0:T(8,128)(2,1)} %param.27) | copy-start | bytes 7962628
  7.2 44.8 %copy-start.14 = (bf16[2,16,3,576]{3,1,2,0:T(8,128)(2,1)S(1)}, bf16[2,16,3,576]{3,1,2,0:T(8,128)(2,1)}, u32[]{:S(2)}) copy-start(bf16[2,16,3,576]{3,1,2,0:T(8,128)(2,1)} %param.33) | copy-start | bytes 331780
  7.2 56.9 %copy-start.18 = (f32[2304]{0:T(1024)S(1)}, f32[2304]{0:T(1024)}, u32[]{:S(2)}) copy-start(f32[2304]{0:T(1024)} %param.24) | copy-start | bytes 27652
  7.2 63.8 %all-gather.3.cloned.1.call-start = ((), (), s32[]{:S(2)}) async-start(), calls=%async_computation.4 | async-start | bytes 5308416 | tf_op jit(solution)/shard_map/all_gather | solution.py:86
  7.9 76.1 %all-gather.5.cloned.1.call-start = ((), (), s32[]{:S(2)}) async-start(), calls=%async_computation.5 | async-start | bytes 1327104 | tf_op jit(solution)/shard_map/all_gather | solution.py:89
  10.4 53.8 %copy-start.7 = (bf16[256,2304]{1,0:T(8,128)(2,1)S(1)}, bf16[256,2304]{1,0:T(8,128)(2,1)}, u32[]{:S(2)}) copy-start(bf16[256,2304]{1,0:T(8,128)(2,1)} %param.18) | copy-start | bytes 3538948
  71.0 2.5 slice-start
  78.0 3.4 copy-start.12
  87.7 56.3 %copy-start.16 = (s32[256,2]{0,1:T(2,128)S(1)}, s32[256,2]{0,1:T(2,128)}, u32[]{:S(2)}) copy-start(s32[256,2]{0,1:T(2,128)} %param.23) | copy-start | bytes 6148
  87.7 53.6 %collective-permute-start = (f32[256,2304]{1,0:T(8,128)S(1)}, f32[256,2304]{1,0:T(8,128)S(1)}, u32[]{:S(2)}, u32[]{:S(2)}) collective-permute-start(f32[256,2304]{1,0:T(8,128)S(1)} %convolution_add_fusion), channel_id=1, source_target_pairs={{0,1},{1,0},{2,3},{3,2},{4,5},{5,4},{6,7},{7,6},{8,9},{9,8},{10,11... | collective-permute-start | bytes 7077896 | tf_op jit(solution)/shard_map/ppermute | solution.py:76
  141.5 9.3 %copy-start.5 = (f32[256,2304]{1,0:T(8,128)}, f32[256,2304]{1,0:T(8,128)S(1)}, u32[]{:S(2)}) copy-start(f32[256,2304]{1,0:T(8,128)S(1)} %add.170) | copy-start | bytes 7077892
  141.5 104.3 %collective-permute-start.1 = (f32[256,2304]{1,0:T(8,128)S(1)}, f32[256,2304]{1,0:T(8,128)}, u32[]{:S(2)}, u32[]{:S(2)}) collective-permute-start(f32[256,2304]{1,0:T(8,128)S(1)} %add.170), channel_id=1, source_target_pairs={{0,2},{1,3},{2,0},{3,1},{4,6},{5,7},{6,4},{7,5},{8,10},{9,11},{10,... | collective-permute-start | bytes 7077896 | tf_op jit(solution)/shard_map/ppermute | solution.py:76
  147.3 105.3 %all-to-all-start.1 = ((bf16[8,1,72]{2,1,0:T(2,128)(2,1)}), bf16[8,1,72]{2,1,0:T(2,128)(2,1)S(1)}, u32[]{:S(2)}, u32[]{:S(2)}) async-start(bf16[8,1,72]{2,1,0:T(2,128)(2,1)} %all_to_all.20), calls=%async_computation.1 | async-start | bytes 8192 | tf_op jit(solution)/shard_map/all_to_all | solution.py:215
  150.8 98.2 %copy-start.17 = (f32[2304]{0:T(1024)S(1)}, f32[2304]{0:T(1024)}, u32[]{:S(2)}) copy-start(f32[2304]{0:T(1024)} %param.25) | copy-start | bytes 27652
  249.0 2.6 copy-start.2
  252.6 8.1 %all-to-all-start.2 = ((bf16[8,72,16]{1,2,0:T(8,128)(2,1)}), bf16[8,72,16]{1,2,0:T(8,128)(2,1)S(1)}, u32[]{:S(2)}, u32[]{:S(2)}) async-start(bf16[8,72,16]{1,2,0:T(8,128)(2,1)} %copy.92), calls=%async_computation.2 | async-start | bytes 65536 | tf_op jit(solution)/shard_map/all_to_all | solution.py:212
  260.7 36.2 %all-to-all-start = ((bf16[8,72,2304]{2,1,0:T(8,128)(2,1)}), bf16[8,72,2304]{2,1,0:T(8,128)(2,1)S(1)}, u32[]{:S(2)}, u32[]{:S(2)}) async-start(bf16[8,72,2304]{2,1,0:T(8,128)(2,1)} %bitcast.55), calls=%async_computation | async-start | bytes 5308416 | tf_op jit(solution)/shard_map/all_to_all | solution.py:209
  296.9 11.4 %copy-start.11 = (bf16[1,256,2,1440]{1,3,2,0:T(8,128)(2,1)S(1)}, bf16[1,256,2,1440]{1,3,2,0:T(8,128)(2,1)}, u32[]{:S(2)}) copy-start(bf16[1,256,2,1440]{1,3,2,0:T(8,128)(2,1)} %param.31) | copy-start | bytes 4423684
  318.8 5.1 %copy-start.4 = (bf16[256,2304]{1,0:T(8,128)(2,1)S(1)}, bf16[256,2304]{1,0:T(8,128)(2,1)}, u32[]{:S(2)}) copy-start(bf16[256,2304]{1,0:T(8,128)(2,1)} %copy-done.3) | copy-start | bytes 3538948
  318.8 5.1 %copy-start.15 = (bf16[2304,8]{0,1:T(8,128)(2,1)S(1)}, bf16[2304,8]{0,1:T(8,128)(2,1)}, u32[]{:S(2)}) copy-start(bf16[2304,8]{0,1:T(8,128)(2,1)} %param.28) | copy-start | bytes 110596
  318.8 37.1 %all-to-all-start.3 = ((bf16[8,72,2304]{2,1,0:T(8,128)(2,1)}), bf16[8,72,2304]{2,1,0:T(8,128)(2,1)}, u32[]{:S(2)}, u32[]{:S(2)}) async-start(bf16[8,72,2304]{2,1,0:T(8,128)(2,1)} %bitcast.152), calls=%async_computation.3 | async-start | bytes 5308416 | tf_op jit(solution)/shard_map/all_to_all | solution.py:242
  323.3 93.7 %all-reduce.2.cloned.1.call-start = ((), (), s32[]{:S(2)}) async-start(), calls=%async_computation.6 | async-start | bytes 2359296 | tf_op jit(solution)/shard_map/psum | solution.py:249
  355.9 7.0 %copy-start.13 = (bf16[256,9,32]{0,2,1:T(8,128)(2,1)S(1)}, bf16[256,9,32]{0,2,1:T(8,128)(2,1)}, u32[]{:S(2)}) copy-start(bf16[256,9,32]{0,2,1:T(8,128)(2,1)} %copy-done.12) | copy-start | bytes 442372
  366.8 53.4 %copy-start.1 = (bf16[576,2304]{1,0:T(8,128)(2,1)S(1)}, bf16[576,2304]{1,0:T(8,128)(2,1)}, u32[]{:S(2)}) copy-start(bf16[576,2304]{1,0:T(8,128)(2,1)} %param.27) | copy-start | bytes 7962628
  (6 other events, 10.2 us)
Sparse Core Ops, SparseCore 0:
  9.9 42.8 all-gather.2
  54.7 24.0 all-gather.4
  361.9 55.0 all-reduce.1
